TPU v7x, 1024 devices: a whole 4x8x16 slice. The times are simulated.
1024 devices in a mesh: node: 256 (over y, x, z_lo, core), local: 4 (over z_hi).
Axes of the slice: x: 4, y: 8, z: 16 (z_hi: 4, z_lo: 4; z = z_hi * 4 + z_lo), core: 2. Of those that a mesh axis runs over, the one named last changes fastest.
Arguments:
- tokens: bfloat16 [131072, 4096], P(('node', 'local')), may hold values from -24 to 24
- queries: bfloat16 [131072, 4096], P(('node', 'local')), may hold values from -6 to 6
- keys: bfloat16 [131072, 512], P(('node', 'local')), may hold values from -6 to 6
- grad_attended: bfloat16 [131072, 4096], P(('node', 'local')), may hold values from -6 to 6
- w_value: bfloat16 [4096, 512], P('local'), may hold values from -0.09375 to 0.09375
Outputs:
- d_keys: bfloat16 [131072, 512], P(('node', 'local'))
- grad_value: float32 [4096, 512], P(('local', 'node'))
All inputs are finite; a program needn't handle non-finite values.
Results may differ from a plain program's by a relative error of at most 0.018.
Values may be sent and summed in bfloat16 or wider, within the bound.
A program may use at most 32 MiB of HBM per device.

v0:
```python
import jax
import jax.numpy as jnp
from jax import lax
from jax.sharding import PartitionSpec as P

HD = 128
KVH = 4
GROUP = 8


def contract_rows(left, right):
    return lax.dot_general(
        left, right, (((0,), (0,)), ((), ())), preferred_element_type=jnp.float32
    )


def rounded(term):
    return lax.optimization_barrier(term.astype(jnp.bfloat16)).astype(jnp.float32)


def attention_grads(queries, keys, grad_attended, values):
    row_count = queries.shape[0]
    head_scale = float(HD) ** (-0.5)
    query_heads = queries.reshape(row_count, KVH, GROUP, HD)
    key_heads = keys.reshape(row_count, KVH, HD)
    value_heads = values.reshape(row_count, KVH, HD)
    upper_heads = grad_attended.reshape(row_count, KVH, GROUP, HD)
    scores = (
        jnp.einsum("tagd,sad->agts", query_heads, key_heads, preferred_element_type=jnp.float32)
        * head_scale
    )
    row_ids = lax.broadcasted_iota(jnp.int32, (row_count, row_count), 0)
    col_ids = lax.broadcasted_iota(jnp.int32, (row_count, row_count), 1)
    scores = jnp.where((col_ids <= row_ids)[None, None], scores, jnp.float32(-1e30))
    row_peak = jnp.max(scores, axis=-1, keepdims=True)
    raised = jnp.exp(scores - row_peak)
    soft_weights = (raised / jnp.sum(raised, axis=-1, keepdims=True)).astype(jnp.bfloat16)
    grad_probs = jnp.einsum(
        "tagd,sad->agts", upper_heads, value_heads, preferred_element_type=jnp.float32
    )
    soft_float = soft_weights.astype(jnp.float32)
    delta = jnp.sum(soft_float * grad_probs, axis=-1, keepdims=True)
    grad_scores = (soft_float * (grad_probs - delta)).astype(jnp.bfloat16)
    d_keys = (
        jnp.einsum("agts,tagd->sad", grad_scores, query_heads, preferred_element_type=jnp.float32)
        * head_scale
    )
    d_keys = d_keys.astype(jnp.bfloat16).reshape(row_count, KVH * HD)
    grad_values = jnp.einsum(
        "agts,tagd->sad", soft_weights, upper_heads, preferred_element_type=jnp.float32
    )
    grad_values = grad_values.astype(jnp.bfloat16).reshape(row_count, KVH * HD)
    return (d_keys, grad_values)


def shards(tokens, queries, keys, grad_attended, w_value):
    row_count = tokens.shape[0]
    full_weight = lax.all_gather(w_value, "local", axis=0, tiled=True)
    values = jnp.dot(tokens, full_weight, preferred_element_type=jnp.float32).astype(jnp.bfloat16)
    d_keys, grad_values = attention_grads(queries, keys, grad_attended, values)
    total_tokens = lax.axis_size("node") * lax.axis_size("local") * row_count
    loss_scale = float(total_tokens) ** (-0.5)
    local_share = lax.psum_scatter(
        rounded(contract_rows(tokens, grad_values) * loss_scale).astype(jnp.bfloat16),
        "local",
        scatter_dimension=0,
        tiled=True,
    ).astype(jnp.float32)
    grad_value = lax.psum_scatter(local_share, "node", scatter_dimension=0, tiled=True)
    return (d_keys, grad_value)


def solution(mesh):
    in_specs = (
        P(("node", "local"), None),
        P(("node", "local"), None),
        P(("node", "local"), None),
        P(("node", "local"), None),
        P("local", None),
    )
    out_specs = (P(("node", "local"), None), P(("local", "node"), None))
    return jax.shard_map(shards, mesh=mesh, in_specs=in_specs, out_specs=out_specs, check_vma=False)
```

profile of v0, /device:TPU:1, one launch (start us, length us, event | category | flops | bytes accessed | tf_op | source)
XLA Modules:
  0.0 1698.9 jit_solution(10651518821869620148)
XLA Ops:
  7.2 0.0 copy-start
  7.2 0.0 all-gather.2.cloned.1.call-start
  7.2 0.7 all-gather.2.cloned.1.call-update
  7.9 0.0 reduce-scatter.3.cloned.1.call-start
  8.0 0.9 reshape.32
  8.9 1.6 copy.39
  10.5 1.6 copy.40
  12.2 2.1 fusion.25
  14.3 171.2 %all-gather.2.cloned.1.call-done = bf16[4096,512]{1,0:T(8,128)(2,1)} async-done(((bf16[1024,512]{1,0:T(8,128)(2,1)}), bf16[4096,512]{1,0:T(8,128)(2,1)}) %all-gather.2.cloned.1.call-update) | async-done | bytes 4194320 | tf_op jit(solution)/shard_map/all_gather | solution.py:58
  185.5 0.0 copy-done
  185.5 2.9 convolution_convert_fusion
  188.5 3.4 fusion.2
  191.9 0.0 copy-start.1
  191.9 0.4 fusion.7
  192.3 0.5 copy-done.1
  192.9 3.2 fusion.1
  196.0 0.0 copy-start.2
  196.0 0.0 reduce-scatter.3.cloned.1.call-update
  196.1 1.4 dynamic-slice
  198.1 0.0 copy-done.2
  198.1 2.0 fusion.6
  200.1 0.8 copy.25
  200.9 127.6 %reduce-scatter.3.cloned.1.call-done = bf16[1024,512]{0,1:T(8,128)(2,1)} async-done(((bf16[4096,512]{0,1:T(8,128)(2,1)}), bf16[1024,512]{0,1:T(8,128)(2,1)}) %reduce-scatter.3.cloned.1.call-update) | async-done | bytes 1048592 | tf_op jit(solution)/shard_map/reduce_scatter | solution.py:63
  328.5 1362.7 %all-reduce.2 = f32[1024,512]{0,1:T(8,128)S(1)} all-reduce(bf16[1024,512]{0,1:T(8,128)(2,1)} %reduce-scatter.3.cloned.1.call-done), channel_id=3, replica_groups=mesh['node'=256,'local'=4] {'node'}, use_global_device_ids=true, to_apply=%region_4.5.clone | all-reduce | flops 524288 | bytes 3145728
  1691.2 0.1 constant_dynamic-slice_fusion
  1691.4 0.7 copy.26
  (2 shorter events, 0.1 us)
Async XLA Ops:
  7.2 178.4 %copy-start = (bf16[128,4096]{1,0:T(8,128)(2,1)S(1)}, bf16[128,4096]{1,0:T(8,128)(2,1)}, u32[]{:S(2)}) copy-start(bf16[128,4096]{1,0:T(8,128)(2,1)} %param.5) | copy-start | bytes 3145732
  7.2 178.3 %all-gather.2.cloned.1.call-start = ((), (), s32[]{:S(2)}) async-start(), calls=%async_computation.1 | async-start | bytes 5242880 | tf_op jit(solution)/shard_map/all_gather | solution.py:58
  7.9 320.6 %reduce-scatter.3.cloned.1.call-start = ((), (), s32[]{:S(2)}) async-start(), calls=%async_computation.2 | async-start | bytes 5242880 | tf_op jit(solution)/shard_map/reduce_scatter | solution.py:63
  191.9 1.0 copy-start.1
  196.0 2.0 copy-start.2
Sparse Core Ops, SparseCore 0:
  10.7 174.7 all-gather.1
  196.2 132.3 reduce-scatter.2
where the time goes:
time: 1700 us
  blocking collectives  1360 us (80%)
  waiting for transfers between devices  300 us (18%)
    unnamed x1, blocking collectives  1360 us
    all_gather x1, waiting for transfers between devices, shards(): full_weight = lax.all_gather(w_value, 'local', axis=0, tiled=True)  171 us
    reduce_scatter x1, waiting for transfers between devices, shards(): lax.psum_scatter(rounded(contract_rows(tokens, grad_values) * loss_scale)...  128 us
  transfers between devices with their start and end apart: 2, of which 2 were waited for; matrix products, arithmetic and copies ran while one was open for 1% of the time, Pallas kernels for 0%

commit v1 on v0

v1 whole, which is shorter than its diff:
```python
import jax
import jax.numpy as jnp
from jax import lax
from jax.experimental import pallas as pl
from jax.experimental.pallas import tpu as pltpu
from jax.sharding import PartitionSpec as P

HD = 128
KVH = 4
GROUP = 8
ROWS = 128
KW = 512
NX, NY, NZL, NZH, NC = 4, 8, 4, 4, 2
NG = NX * NC
MESH = pl.DeviceIdType.MESH
F32 = jnp.float32
BF16 = jnp.bfloat16


def node_of(y, x, z_lo, core):
    return ((y * NX + x) * NZL + z_lo) * NC + core


def over_rows(left, right):
    return lax.dot_general(left, right, (((0,), (0,)), ((), ())), preferred_element_type=F32)


def over_columns(left, right):
    return lax.dot_general(left, right, (((1,), (1,)), ((), ())), preferred_element_type=F32)


def stacked(ref, a):
    return jnp.concatenate(
        [ref[:, (a * GROUP + g) * HD : (a * GROUP + g + 1) * HD] for g in range(GROUP)], axis=0
    )


def kernel(
    tok_hbm, q_hbm, k_hbm, g_hbm, w_hbm, dk_ref, gw_ref,
    tok, q, k, g, w_own, w_far, soft, tok_group, gv_group, part_send, part_recv,
    fin_send, fin_recv, load_sem, send_sem, recv_sem, *, loss_scale,
):
    node, z_hi = lax.axis_index("node"), lax.axis_index("local")
    core = lax.rem(node, NC)
    z_lo = lax.rem(node // NC, NZL)
    x = lax.rem(node // (NC * NZL), NX)
    y = node // (NC * NZL * NX)
    z = z_hi * NZL + z_lo
    p = x * NC + core
    head_scale = float(HD) ** -0.5

    def device(y_, x_, core_):
        return (node_of(y_, x_, z_lo, core_), z_hi)

    sibling = device(y, x, 1 - core)
    x_peers = [lax.rem(x + d, NX) for d in range(1, NX)]
    y_peers = [lax.rem(y + d, NY) for d in range(1, NY)]
    far_peers = [lax.rem(z_hi + d, NZH) for d in range(1, NZH)]

    loads = [
        pltpu.make_async_copy(src, dst, load_sem.at[i])
        for i, (src, dst) in enumerate(
            [(q_hbm, q), (k_hbm, k), (g_hbm, g), (tok_hbm, tok), (w_hbm, w_own)]
        )
    ]
    for load in loads:
        load.start()

    barrier = pltpu.get_barrier_semaphore()

    def greet(device_id):
        pl.semaphore_signal(barrier, inc=1, device_id=device_id, device_id_type=MESH)

    greet(sibling)
    for x_ in x_peers:
        for core_ in (core, 1 - core):
            greet(device(y, x_, core_))
    for y_ in y_peers:
        greet(device(y_, x, core))
    for h in far_peers:
        greet((node, h))
    giver_y, giver_x, giver_core = x * 2 + z_lo // 2, y // 2, lax.rem(y, 2)
    takes_own = (giver_y == y) & (giver_x == x) & (giver_core == core)
    for z_ in range(NZH * NZL):
        giver = (node_of(giver_y, giver_x, z_ % NZL, giver_core), z_ // NZL)

        @pl.when(jnp.logical_not(takes_own & (z == z_)))
        def _():
            greet(giver)

    near = 1 + 2 * (NX - 1) + (NY - 1) + (NZH - 1)
    pl.semaphore_wait(barrier, near + NZH * NZL - jnp.where(takes_own, 1, 0))

    def send(src, dst, phase, device_id):
        pltpu.make_async_remote_copy(
            src_ref=src, dst_ref=dst, send_sem=send_sem.at[phase], recv_sem=recv_sem.at[phase],
            device_id=device_id, device_id_type=MESH,
        ).start()

    def wait(ref, sem):
        pltpu.make_async_copy(ref, ref, sem).wait()

    W_Z, W_Y, W_X, W_C, TOK, GV_X, GV_OWN, GV_C, PART, FIN = range(10)

    piece = (core * NX + x) * NY + y
    for d, h in enumerate(far_peers):
        send(
            w_hbm.at[pl.ds(pl.multiple_of(piece * 16, 16), 16)],
            w_far.at[piece, NZH - 2 - d], W_Z, (node, h),
        )

    def columns(zh, p_):
        return tok_hbm.at[:, pl.ds(pl.multiple_of(zh * (NG * HD) + p_ * HD, HD), HD)]

    for x_, core_ in [(x, 1 - core)] + [(x_, c_) for x_ in x_peers for c_ in (core, 1 - core)]:
        for zh in range(NZH):
            send(
                columns(zh, x_ * NC + core_), tok_group.at[p, :, zh * HD : (zh + 1) * HD], TOK,
                device(y, x_, core_),
            )
    for zh in range(NZH):
        pltpu.make_async_copy(
            columns(zh, p), tok_group.at[p, :, zh * HD : (zh + 1) * HD], recv_sem.at[TOK]
        ).start()

    row_ids = lax.broadcasted_iota(jnp.int32, (GROUP, ROWS, ROWS), 1).reshape(GROUP * ROWS, ROWS)
    col_ids = lax.broadcasted_iota(jnp.int32, (GROUP * ROWS, ROWS), 1)
    allowed = col_ids <= row_ids

    def softmax_head(a):
        cols = slice(a * HD, (a + 1) * HD)
        scores = over_columns(stacked(q, a), k[:, cols]) * head_scale
        scores = jnp.where(allowed, scores, F32(-1e30))
        raised = jnp.exp(scores - jnp.max(scores, axis=-1, keepdims=True))
        weights = (raised / jnp.sum(raised, axis=-1, keepdims=True)).astype(BF16)
        soft[a] = weights
        gv_group[p, :, cols] = over_rows(weights, stacked(g, a)).astype(BF16)

    for load in loads[:3]:
        load.wait()
    softmax_head(0)
    softmax_head(1)
    wait(w_far.at[0], recv_sem.at[W_Z])
    for y_ in y_peers:
        send(w_far.at[piece], w_far.at[piece], W_Y, device(y_, x, core))
    softmax_head(2)
    softmax_head(3)

    for x_ in x_peers:
        send(gv_group.at[p], gv_group.at[p], GV_X, device(y, x_, core))
    send(gv_group.at[p], gv_group.at[p], GV_OWN, sibling)
    wait(w_far.at[0 : NY - 1], recv_sem.at[W_Y])
    plane = pl.ds((core * NX + x) * NY, NY)
    for x_ in x_peers:
        send(w_far.at[plane], w_far.at[plane], W_X, device(y, x_, core))
    loads[3].wait()
    loads[4].wait()
    own_columns = pl.ds(pl.multiple_of(z_hi * (NG * HD), HD), NG * HD)
    total = jnp.dot(tok[:, own_columns], w_own[...], preferred_element_type=F32)
    wait(gv_group.at[0 : NX - 1], recv_sem.at[GV_X])
    for x_ in x_peers:
        send(gv_group.at[x_ * NC + core], gv_group.at[x_ * NC + core], GV_C, sibling)
    wait(tok_group, recv_sem.at[TOK])
    wait(gv_group.at[0], recv_sem.at[GV_OWN])
    wait(gv_group.at[0 : NX - 1], recv_sem.at[GV_C])

    gv_all = gv_group[...].reshape(NG * ROWS, KW)
    for zh in range(NZH):
        lanes = slice(zh * HD, (zh + 1) * HD)
        tok_all = tok_group[:, :, lanes].reshape(NG * ROWS, HD)
        term = over_rows(tok_all, gv_all) * loss_scale
        part_send[:, zh] = term.astype(BF16).reshape(NY, 16, KW)
    for y_ in y_peers:
        send(part_send.at[y_], part_recv.at[y], PART, device(y_, x, core))
    pltpu.make_async_copy(part_send.at[y], part_recv.at[y], recv_sem.at[PART]).start()
    wait(part_recv, recv_sem.at[PART])
    part = part_recv[0].astype(F32)
    for y_ in range(1, NY):
        part = part + part_recv[y_].astype(F32)
    part = part.reshape(64, KW)
    for j in range(16):
        fin_send[j] = part[4 * j : 4 * j + 4]
    gives_own = (lax.rem(y, 2) == z_lo // 2) & (y // 2 == x) & (x * NC + core == y)
    for j in range(16):
        zh, zl1, core_ = j // 4, (j // 2) % 2, j % 2
        z_lo_ = lax.rem(y, 2) * 2 + zl1
        owner = (node_of(x * NC + core, y // 2, z_lo_, core_), zh)
        own = gives_own & (z_hi == zh) & (z_lo == z_lo_) & (core == core_)

        @pl.when(own)
        def _():
            pltpu.make_async_copy(fin_send.at[j], fin_recv.at[z], recv_sem.at[FIN]).start()

        @pl.when(jnp.logical_not(own))
        def _():
            send(fin_send.at[j], fin_recv.at[z], FIN, owner)

    wait(w_far.at[0 : (NX - 1) * NY], recv_sem.at[W_X])
    half = pl.ds(core * (NX * NY), NX * NY)
    send(w_far.at[half], w_far.at[half], W_C, sibling)
    wait(w_far.at[0 : NX * NY], recv_sem.at[W_C])
    for d in range(NZH - 1):
        h = far_peers[d]
        cols = pl.ds(pl.multiple_of(h * (NG * HD), HD), NG * HD)
        w_h = w_far[:, d].reshape(NG * HD, KW)
        total = total + jnp.dot(tok[:, cols], w_h, preferred_element_type=F32)
    values = total.astype(BF16)
    for a in range(KVH):
        cols = slice(a * HD, (a + 1) * HD)
        grad_probs = over_columns(stacked(g, a), values[:, cols])
        soft_float = soft[a].astype(F32)
        delta = jnp.sum(soft_float * grad_probs, axis=-1, keepdims=True)
        grad_scores = (soft_float * (grad_probs - delta)).astype(BF16)
        dk_ref[:, cols] = (over_rows(grad_scores, stacked(q, a)) * head_scale).astype(BF16)

    wait(fin_recv, recv_sem.at[FIN])
    out = fin_recv[0]
    for z_ in range(1, NZH * NZL):
        out = out + fin_recv[z_]
    gw_ref[...] = out

    wait(w_far.at[0], send_sem.at[W_Z])
    wait(w_far.at[0 : NY - 1], send_sem.at[W_Y])
    wait(w_far.at[0 : (NX - 1) * NY], send_sem.at[W_X])
    wait(w_far.at[0 : NX * NY], send_sem.at[W_C])
    wait(tok_group.at[0 : NG - 1], send_sem.at[TOK])
    wait(gv_group.at[0 : NX - 1], send_sem.at[GV_X])
    wait(gv_group.at[0], send_sem.at[GV_OWN])
    wait(gv_group.at[0 : NX - 1], send_sem.at[GV_C])
    wait(part_send.at[0 : NY - 1], send_sem.at[PART])
    wait(fin_send.at[0:15], send_sem.at[FIN])

    @pl.when(jnp.logical_not(gives_own))
    def _():
        wait(fin_send.at[0], send_sem.at[FIN])


def shards(tokens, queries, keys, grad_attended, w_value):
    total_tokens = lax.axis_size("node") * lax.axis_size("local") * tokens.shape[0]
    loss_scale = float(total_tokens) ** -0.5

    def body(*refs):
        kernel(*refs, loss_scale=loss_scale)

    return pl.pallas_call(
        body,
        out_shape=(
            jax.ShapeDtypeStruct((ROWS, KW), BF16),
            jax.ShapeDtypeStruct((4, KW), F32),
        ),
        in_specs=[pl.BlockSpec(memory_space=pl.ANY)] * 5,
        out_specs=(pl.BlockSpec(memory_space=pltpu.VMEM),) * 2,
        scratch_shapes=[
            pltpu.VMEM((ROWS, 4096), BF16),
            pltpu.VMEM((ROWS, 4096), BF16),
            pltpu.VMEM((ROWS, KW), BF16),
            pltpu.VMEM((ROWS, 4096), BF16),
            pltpu.VMEM((1024, KW), BF16),
            pltpu.VMEM((64, NZH - 1, 16, KW), BF16),
            pltpu.VMEM((KVH, GROUP * ROWS, ROWS), BF16),
            pltpu.VMEM((NG, ROWS, KW), BF16),
            pltpu.VMEM((NG, ROWS, KW), BF16),
            pltpu.VMEM((NY, NZH, 16, KW), BF16),
            pltpu.VMEM((NY, NZH, 16, KW), BF16),
            pltpu.VMEM((16, 4, KW), F32),
            pltpu.VMEM((16, 4, KW), F32),
            pltpu.SemaphoreType.DMA((5,)),
            pltpu.SemaphoreType.DMA((10,)),
            pltpu.SemaphoreType.DMA((10,)),
        ],
        compiler_params=pltpu.CompilerParams(
            collective_id=0, has_side_effects=True, vmem_limit_bytes=48 * 1024 * 1024
        ),
        cost_estimate=pl.CostEstimate(
            flops=1_700_000_000, bytes_accessed=5_000_000, transcendentals=524_288
        ),
    )(tokens, queries, keys, grad_attended, w_value)


def solution(mesh):
    in_specs = (
        P(("node", "local"), None),
        P(("node", "local"), None),
        P(("node", "local"), None),
        P(("node", "local"), None),
        P("local", None),
    )
    out_specs = (P(("node", "local"), None), P(("local", "node"), None))
    return jax.shard_map(shards, mesh=mesh, in_specs=in_specs, out_specs=out_specs, check_vma=False)
```

time: 1700 us -> 84.3 us (0.05)
  the two profiles are of different devices: /device:TPU:1 before, /device:TPU:7 now
where the time goes in v1:
time: 84.3 us; the launch traced here: 84 us
  Pallas kernels  76.3 us (91%)
  local copies, waits for them, and re-layouts  7.05 us (8%)
    pallas_call x1, Pallas kernels, shards(): pl.pallas_call(body, out_shape=(jax.ShapeDtypeStruct((ROWS, KW), BF16), j...  76.3 us
    unnamed x12, local copies, waits for them, and re-layouts  7.05 us

profile of v1, /device:TPU:7, one launch (start us, length us, event | category | flops | bytes accessed | tf_op | source)
XLA Modules:
  0.0 84.0 jit_solution(18043519538854853292)
XLA Ops:
  0.6 0.0 copy-start
  0.6 1.2 %copy-done = bf16[128,4096]{1,0:T(8,128)(2,1)S(1)} copy-done((bf16[128,4096]{1,0:T(8,128)(2,1)S(1)}, bf16[128,4096]{1,0:T(8,128)(2,1)}, u32[]{:S(2)}) %copy-start) | copy-done | bytes 1048600
  1.9 0.0 copy-start.1
  1.9 1.2 %copy-done.1 = bf16[128,4096]{1,0:T(8,128)(2,1)S(1)} copy-done((bf16[128,4096]{1,0:T(8,128)(2,1)S(1)}, bf16[128,4096]{1,0:T(8,128)(2,1)}, u32[]{:S(2)}) %copy-start.1) | copy-done | bytes 1048600
  3.1 0.0 copy-start.2
  3.1 1.2 %copy-done.2 = bf16[128,4096]{1,0:T(8,128)(2,1)S(1)} copy-done((bf16[128,4096]{1,0:T(8,128)(2,1)S(1)}, bf16[128,4096]{1,0:T(8,128)(2,1)}, u32[]{:S(2)}) %copy-start.2) | copy-done | bytes 1048600
  4.3 0.0 copy-start.3
  4.3 1.2 %copy-done.3 = bf16[1024,512]{1,0:T(8,128)(2,1)S(1)} copy-done((bf16[1024,512]{1,0:T(8,128)(2,1)S(1)}, bf16[1024,512]{1,0:T(8,128)(2,1)}, u32[]{:S(2)}) %copy-start.3) | copy-done | bytes 1048600
  5.5 0.0 copy-start.4
  5.5 0.9 %copy-done.4 = bf16[128,512]{1,0:T(8,128)(2,1)S(1)} copy-done((bf16[128,512]{1,0:T(8,128)(2,1)S(1)}, bf16[128,512]{1,0:T(8,128)(2,1)}, u32[]{:S(2)}) %copy-start.4) | copy-done | bytes 131096
  6.4 76.3 %shard_map.68 = (bf16[128,512]{1,0:T(8,128)(2,1)S(1)}, f32[4,512]{1,0:T(4,128)S(1)}) custom-call(bf16[128,4096]{1,0:T(8,128)(2,1)S(1)} %copy-done, bf16[128,4096]{1,0:T(8,128)(2,1)S(1)} %copy-done.1, bf16[128,512]{1,0:T(8,128)(2,1)S(1)} %copy-done.4, bf16[128,4096]{1,0:T(8,128)(2,1)S(1)} %copy-done.2, bf16[1024,512]{1,0:T(8,128)(2,1)S(1)} %copy-done.3), custom_call_target="tpu_custom_call" | custom-call | flops 1700000000 | bytes 5000000 | tf_op jit(solution)/shard_map/pallas_call | solution.py:245
  82.8 0.7 copy.9
  83.4 0.6 copy.10
Async XLA Ops:
  0.6 1.2 %copy-start = (bf16[128,4096]{1,0:T(8,128)(2,1)S(1)}, bf16[128,4096]{1,0:T(8,128)(2,1)}, u32[]{:S(2)}) copy-start(bf16[128,4096]{1,0:T(8,128)(2,1)} %refs_0_.1) | copy-start | bytes 3145732
  1.9 1.2 %copy-start.1 = (bf16[128,4096]{1,0:T(8,128)(2,1)S(1)}, bf16[128,4096]{1,0:T(8,128)(2,1)}, u32[]{:S(2)}) copy-start(bf16[128,4096]{1,0:T(8,128)(2,1)} %refs_1_.1) | copy-start | bytes 3145732
  3.1 1.2 %copy-start.2 = (bf16[128,4096]{1,0:T(8,128)(2,1)S(1)}, bf16[128,4096]{1,0:T(8,128)(2,1)}, u32[]{:S(2)}) copy-start(bf16[128,4096]{1,0:T(8,128)(2,1)} %refs_3_.1) | copy-start | bytes 3145732
  4.3 1.2 %copy-start.3 = (bf16[1024,512]{1,0:T(8,128)(2,1)S(1)}, bf16[1024,512]{1,0:T(8,128)(2,1)}, u32[]{:S(2)}) copy-start(bf16[1024,512]{1,0:T(8,128)(2,1)} %refs_4_.1) | copy-start | bytes 3145732
  5.5 0.9 %copy-start.4 = (bf16[128,512]{1,0:T(8,128)(2,1)S(1)}, bf16[128,512]{1,0:T(8,128)(2,1)}, u32[]{:S(2)}) copy-start(bf16[128,512]{1,0:T(8,128)(2,1)} %refs_2_.1) | copy-start | bytes 393220

commit v2 on v1

v2 whole, which is shorter than its diff:
```python
import jax
import jax.numpy as jnp
from jax import lax
from jax.experimental import pallas as pl
from jax.experimental.pallas import tpu as pltpu
from jax.sharding import PartitionSpec as P

HD = 128
KVH = 4
GROUP = 8
ROWS = 128
KW = 512
NX, NY, NZL, NZH, NC = 4, 8, 4, 4, 2
NG = NX * NC
W_Z, W_Y, GV_X, GV_OWN, GV_C, PAIR, VAL, FIN, TOK, PART = 0, 1, 2, 3, 4, 5, 6, 7, 8, 12
MESH = pl.DeviceIdType.MESH
F32 = jnp.float32
BF16 = jnp.bfloat16


def node_of(y, x, z_lo, core):
    return ((y * NX + x) * NZL + z_lo) * NC + core


def over_rows(left, right):
    return lax.dot_general(left, right, (((0,), (0,)), ((), ())), preferred_element_type=F32)


def over_columns(left, right):
    return lax.dot_general(left, right, (((1,), (1,)), ((), ())), preferred_element_type=F32)


def stacked(ref, a):
    return jnp.concatenate(
        [ref[:, (a * GROUP + g) * HD : (a * GROUP + g + 1) * HD] for g in range(GROUP)], axis=0
    )


def kernel(
    tok_hbm, q_hbm, k_hbm, g_hbm, w_hbm, dk_ref, gw_ref,
    q, k, g, w_far, w_cat, soft, tok_group, gv_group, part_send, part_recv,
    fin_send, fin_recv, pair_send, pair_recv, val_send, val_recv,
    load_sem, send_sem, recv_sem, *, loss_scale,
):
    node, z_hi = lax.axis_index("node"), lax.axis_index("local")
    core = lax.rem(node, NC)
    z_lo = lax.rem(node // NC, NZL)
    x = lax.rem(node // (NC * NZL), NX)
    y = node // (NC * NZL * NX)
    z = z_hi * NZL + z_lo
    p = x * NC + core
    head_scale = float(HD) ** -0.5

    def device(y_, x_, core_):
        return (node_of(y_, x_, z_lo, core_), z_hi)

    sibling = device(y, x, 1 - core)
    x_peers = [lax.rem(x + d, NX) for d in range(1, NX)]
    y_peers = [lax.rem(y + d, NY) for d in range(1, NY)]
    far_peers = [lax.rem(z_hi + d, NZH) for d in range(1, NZH)]

    own_rows = w_hbm.at[pl.ds(pl.multiple_of(p * HD, HD), HD)]
    loads = [
        pltpu.make_async_copy(src, dst, load_sem.at[i])
        for i, (src, dst) in enumerate(
            [(q_hbm, q), (k_hbm, k), (g_hbm, g), (own_rows, w_cat.at[z_hi])]
        )
    ]
    for load in loads:
        load.start()

    barrier = pltpu.get_barrier_semaphore()

    def greet(device_id):
        pl.semaphore_signal(barrier, inc=1, device_id=device_id, device_id_type=MESH)

    giver_y, giver_x, giver_core = x * 2 + z_lo // 2, y // 2, lax.rem(y, 2)
    takes_own = (giver_y == y) & (giver_x == x) & (giver_core == core)
    for z_ in range(NZH * NZL):
        giver = (node_of(giver_y, giver_x, z_ % NZL, giver_core), z_ // NZL)

        @pl.when(jnp.logical_not(takes_own & (z == z_)))
        def _():
            greet(giver)

    for h in far_peers:
        greet((node, h))
    for y_ in y_peers:
        greet(device(y_, x, core))
    for x_ in x_peers:
        for core_ in (core, 1 - core):
            greet(device(y, x_, core_))
    greet(sibling)
    near = 1 + 2 * (NX - 1) + (NY - 1) + (NZH - 1)
    pl.semaphore_wait(barrier, near + NZH * NZL - jnp.where(takes_own, 1, 0))

    def send(src, dst, phase, device_id):
        pltpu.make_async_remote_copy(
            src_ref=src, dst_ref=dst, send_sem=send_sem.at[phase], recv_sem=recv_sem.at[phase],
            device_id=device_id, device_id_type=MESH,
        ).start()

    def wait(ref, sem):
        pltpu.make_async_copy(ref, ref, sem).wait()

    piece = w_hbm.at[pl.ds(pl.multiple_of(p * HD + y * 16, 16), 16)]
    for d, h in enumerate(far_peers):
        send(piece, w_far.at[y, NZH - 2 - d], W_Z, (node, h))

    def columns(zh, p_):
        return tok_hbm.at[:, pl.ds(pl.multiple_of(zh * (NG * HD) + p_ * HD, HD), HD)]

    def swap_tokens(zh):
        for x_ in x_peers:
            for core_ in (core, 1 - core):
                send(
                    columns(zh, x_ * NC + core_), tok_group.at[zh, p], TOK + zh,
                    device(y, x_, core_),
                )
        send(columns(zh, x * NC + 1 - core), tok_group.at[zh, p], TOK + zh, sibling)
        pltpu.make_async_copy(columns(zh, p), tok_group.at[zh, p], recv_sem.at[TOK + zh]).start()

    swap_tokens(0)
    swap_tokens(1)

    row_ids = lax.broadcasted_iota(jnp.int32, (GROUP, ROWS, ROWS), 1).reshape(GROUP * ROWS, ROWS)
    col_ids = lax.broadcasted_iota(jnp.int32, (GROUP * ROWS, ROWS), 1)
    allowed = col_ids <= row_ids

    def softmax_head(a):
        cols = slice(a * HD, (a + 1) * HD)
        scores = over_columns(stacked(q, a), k[:, cols]) * head_scale
        scores = jnp.where(allowed, scores, F32(-1e30))
        raised = jnp.exp(scores - jnp.max(scores, axis=-1, keepdims=True))
        weights = (raised / jnp.sum(raised, axis=-1, keepdims=True)).astype(BF16)
        soft[a] = weights
        gv_group[p, :, cols] = over_rows(weights, stacked(g, a)).astype(BF16)

    for load in loads[:3]:
        load.wait()
    softmax_head(0)
    softmax_head(1)
    wait(w_far.at[0], recv_sem.at[W_Z])
    for y_ in y_peers:
        send(w_far.at[y], w_far.at[y], W_Y, device(y_, x, core))
    softmax_head(2)
    softmax_head(3)

    for x_ in x_peers:
        send(gv_group.at[p], gv_group.at[p], GV_X, device(y, x_, core))
    send(gv_group.at[p], gv_group.at[p], GV_OWN, sibling)
    swap_tokens(2)
    swap_tokens(3)
    wait(gv_group.at[0 : NX - 1], recv_sem.at[GV_X])
    for x_ in x_peers:
        send(gv_group.at[x_ * NC + core], gv_group.at[x_ * NC + core], GV_C, sibling)
    wait(gv_group.at[0], recv_sem.at[GV_OWN])
    wait(gv_group.at[0 : NX - 1], recv_sem.at[GV_C])

    gv_all = gv_group[...].reshape(NG * ROWS, KW)
    for zh in range(NZH):
        wait(tok_group.at[zh], recv_sem.at[TOK + zh])
        term = over_rows(tok_group[zh].reshape(NG * ROWS, HD), gv_all) * loss_scale
        part_send[zh] = term.astype(BF16).reshape(NY, 16, KW)
        for y_ in y_peers:
            send(part_send.at[zh, y_], part_recv.at[zh, y], PART + zh, device(y_, x, core))
        pltpu.make_async_copy(
            part_send.at[zh, y], part_recv.at[zh, y], recv_sem.at[PART + zh]
        ).start()

    wait(w_far.at[0 : NY - 1], recv_sem.at[W_Y])
    loads[3].wait()
    for d, h in enumerate(far_peers):
        w_cat[h] = w_far[:, d].reshape(HD, KW)

    def partial_values(core_):
        total = None
        for zh in range(NZH):
            left = jnp.concatenate([tok_group[zh, x_ * NC + core_] for x_ in range(NX)], axis=0)
            product = jnp.dot(left, w_cat[zh], preferred_element_type=F32)
            total = product if total is None else total + product
        return total.reshape(NX, ROWS, KW)

    pair_send[...] = partial_values(1 - core).astype(BF16)
    send(pair_send, pair_recv, PAIR, sibling)
    val_send[...] = partial_values(core)

    gives_own = (lax.rem(y, 2) == z_lo // 2) & (y // 2 == x) & (x * NC + core == y)

    def finish(zh):
        wait(part_recv.at[zh], recv_sem.at[PART + zh])
        part = part_recv[zh, 0].astype(F32)
        for y_ in range(1, NY):
            part = part + part_recv[zh, y_].astype(F32)
        for i in range(4):
            j = zh * 4 + i
            rows = part[4 * i : 4 * i + 4]
            fin_send[j] = jnp.concatenate(
                [rows[:, c * HD : (c + 1) * HD] for c in range(KW // HD)], axis=0
            ).astype(BF16)
            z_lo_, core_ = lax.rem(y, 2) * 2 + i // 2, i % 2
            owner = (node_of(x * NC + core, y // 2, z_lo_, core_), zh)
            own = gives_own & (z_hi == zh) & (z_lo == z_lo_) & (core == core_)

            @pl.when(own)
            def _():
                pltpu.make_async_copy(fin_send.at[j], fin_recv.at[z], recv_sem.at[FIN]).start()

            @pl.when(jnp.logical_not(own))
            def _():
                send(fin_send.at[j], fin_recv.at[z], FIN, owner)

    finish(0)
    wait(pair_recv, recv_sem.at[PAIR])
    for x_ in range(NX):
        summed = val_send[x_] + pair_recv[x_].astype(F32)
        val_send[x_] = summed
        val_out = summed.astype(BF16)
        pair_recv[x_] = val_out
    for x_ in x_peers:
        send(pair_recv.at[x_], val_recv.at[x], VAL, device(y, x_, core))
    finish(1)
    finish(2)
    finish(3)

    wait(val_recv.at[0 : NX - 1], recv_sem.at[VAL])
    total = val_send[x]
    for x_ in x_peers:
        total = total + val_recv[x_].astype(F32)
    values = total.astype(BF16)
    for a in range(KVH):
        cols = slice(a * HD, (a + 1) * HD)
        grad_probs = over_columns(stacked(g, a), values[:, cols])
        soft_float = soft[a].astype(F32)
        delta = jnp.sum(soft_float * grad_probs, axis=-1, keepdims=True)
        grad_scores = (soft_float * (grad_probs - delta)).astype(BF16)
        dk_ref[:, cols] = (over_rows(grad_scores, stacked(q, a)) * head_scale).astype(BF16)

    wait(fin_recv, recv_sem.at[FIN])
    out = fin_recv[0].astype(F32)
    for z_ in range(1, NZH * NZL):
        out = out + fin_recv[z_].astype(F32)
    for c in range(KW // HD):
        gw_ref[:, c * HD : (c + 1) * HD] = out[4 * c : 4 * c + 4]

    wait(w_far.at[0], send_sem.at[W_Z])
    wait(w_far.at[0 : NY - 1], send_sem.at[W_Y])
    for zh in range(NZH):
        wait(tok_group.at[zh, 0 : NG - 1], send_sem.at[TOK + zh])
        wait(part_send.at[zh, 0 : NY - 1], send_sem.at[PART + zh])
    wait(gv_group.at[0 : NX - 1], send_sem.at[GV_X])
    wait(gv_group.at[0], send_sem.at[GV_OWN])
    wait(gv_group.at[0 : NX - 1], send_sem.at[GV_C])
    wait(pair_send, send_sem.at[PAIR])
    wait(val_recv.at[0 : NX - 1], send_sem.at[VAL])
    wait(fin_send.at[0:15], send_sem.at[FIN])

    @pl.when(jnp.logical_not(gives_own))
    def _():
        wait(fin_send.at[0], send_sem.at[FIN])


def shards(tokens, queries, keys, grad_attended, w_value):
    total_tokens = lax.axis_size("node") * lax.axis_size("local") * tokens.shape[0]
    loss_scale = float(total_tokens) ** -0.5

    def body(*refs):
        kernel(*refs, loss_scale=loss_scale)

    return pl.pallas_call(
        body,
        out_shape=(
            jax.ShapeDtypeStruct((ROWS, KW), BF16),
            jax.ShapeDtypeStruct((4, KW), F32),
        ),
        in_specs=[pl.BlockSpec(memory_space=pl.ANY)] * 5,
        out_specs=(pl.BlockSpec(memory_space=pltpu.VMEM),) * 2,
        scratch_shapes=[
            pltpu.VMEM((ROWS, 4096), BF16),
            pltpu.VMEM((ROWS, KW), BF16),
            pltpu.VMEM((ROWS, 4096), BF16),
            pltpu.VMEM((NY, NZH - 1, 16, KW), BF16),
            pltpu.VMEM((NZH, HD, KW), BF16),
            pltpu.VMEM((KVH, GROUP * ROWS, ROWS), BF16),
            pltpu.VMEM((NZH, NG, ROWS, HD), BF16),
            pltpu.VMEM((NG, ROWS, KW), BF16),
            pltpu.VMEM((NZH, NY, 16, KW), BF16),
            pltpu.VMEM((NZH, NY, 16, KW), BF16),
            pltpu.VMEM((16, 16, HD), BF16),
            pltpu.VMEM((16, 16, HD), BF16),
            pltpu.VMEM((NX, ROWS, KW), BF16),
            pltpu.VMEM((NX, ROWS, KW), BF16),
            pltpu.VMEM((NX, ROWS, KW), F32),
            pltpu.VMEM((NX, ROWS, KW), BF16),
            pltpu.SemaphoreType.DMA((4,)),
            pltpu.SemaphoreType.DMA((16,)),
            pltpu.SemaphoreType.DMA((16,)),
        ],
        compiler_params=pltpu.CompilerParams(
            collective_id=0, has_side_effects=True, vmem_limit_bytes=60 * 1024 * 1024
        ),
        cost_estimate=pl.CostEstimate(
            flops=1_700_000_000, bytes_accessed=5_000_000, transcendentals=524_288
        ),
    )(tokens, queries, keys, grad_attended, w_value)


def solution(mesh):
    in_specs = (
        P(("node", "local"), None),
        P(("node", "local"), None),
        P(("node", "local"), None),
        P(("node", "local"), None),
        P("local", None),
    )
    out_specs = (P(("node", "local"), None), P(("local", "node"), None))
    return jax.shard_map(shards, mesh=mesh, in_specs=in_specs, out_specs=out_specs, check_vma=False)
```

time: 84.3 us -> 67.9 us (0.81)
  the two profiles are of different devices: /device:TPU:7 before, /device:TPU:1 now
where the time goes in v2:
time: 67.9 us; the launch traced here: 67.7 us
  Pallas kernels  64.9 us (96%)
  local copies, waits for them, and re-layouts  2.18 us (3%)
    pallas_call x1, Pallas kernels, shards(): pl.pallas_call(body, out_shape=(jax.ShapeDtypeStruct((ROWS, KW), BF16), j...  64.9 us
    unnamed x4, local copies, waits for them, and re-layouts  2.18 us

profile of v2, /device:TPU:1, one launch (start us, length us, event | category | flops | bytes accessed | tf_op | source)
XLA Modules:
  0.0 67.7 jit_solution(13116277917829048274)
XLA Ops:
  0.6 64.9 %shard_map.68 = (bf16[128,512]{1,0:T(8,128)(2,1)}, f32[4,512]{1,0:T(4,128)}) custom-call(bf16[128,4096]{1,0:T(8,128)(2,1)} %refs_0_.1, bf16[128,4096]{1,0:T(8,128)(2,1)} %refs_1_.1, bf16[128,512]{1,0:T(8,128)(2,1)} %refs_2_.1, bf16[128,4096]{1,0:T(8,128)(2,1)} %refs_3_.1, bf16[1024,512]{1,0:T(8,128)(2,1)} %refs_4_.1), custom_call_target="tpu_custom_call" | custom-call | flops 1700000000 | bytes 5000000 | tf_op jit(solution)/shard_map/pallas_call | solution.py:270
  65.6 0.0 copy-start
  65.6 1.6 %copy.9 = bf16[128,512]{1,0:T(8,128)(2,1)} copy(bf16[128,512]{1,0:T(8,128)(2,1)} %get-tuple-element.4) | data formatting | bytes 262144
  67.1 0.0 copy-done
  67.1 0.6 copy.10
Async XLA Ops:
  65.6 1.6 %copy-start = (f32[4,512]{1,0:T(4,128)S(1)}, f32[4,512]{1,0:T(4,128)}, u32[]{:S(2)}) copy-start(f32[4,512]{1,0:T(4,128)} %get-tuple-element.5) | copy-start | bytes 24580

commit v3 on v2

v3 whole, which is shorter than its diff:
```python
import jax
import jax.numpy as jnp
from jax import lax
from jax.experimental import pallas as pl
from jax.experimental.pallas import tpu as pltpu
from jax.sharding import PartitionSpec as P

HD = 128
KVH = 4
GROUP = 8
ROWS = 128
KW = 512
NX, NY, NZL, NZH, NC = 4, 8, 4, 4, 2
NG = NX * NC
W_Z, W_Y, FIN, GV_X, GV_OWN, GV_C, VAL, TOK, PART, PAIR = 0, 1, 2, 3, 5, 7, 9, 11, 15, 19
LOG2_E = 1.4426950408889634
MESH = pl.DeviceIdType.MESH
F32 = jnp.float32
BF16 = jnp.bfloat16


def node_of(y, x, z_lo, core):
    return ((y * NX + x) * NZL + z_lo) * NC + core


def over_columns(left, right):
    return lax.dot_general(left, right, (((1,), (1,)), ((), ())), preferred_element_type=F32)


def stacked(ref, a):
    return jnp.concatenate(
        [ref[:, (a * GROUP + g) * HD : (a * GROUP + g + 1) * HD] for g in range(GROUP)], axis=0
    )


def kernel(
    tok_hbm, q_hbm, k_hbm, g_hbm, w_hbm, dk_ref, gw_ref,
    q, k, g, w_far, w_cat, soft, tok_group, tok_turned, gv_group, part_send, part_recv,
    fin_send, fin_recv, pair_send, pair_recv, val_own, val_other, val_send, val_recv,
    load_sem, send_sem, recv_sem, *, loss_scale,
):
    node, z_hi = lax.axis_index("node"), lax.axis_index("local")
    core = lax.rem(node, NC)
    z_lo = lax.rem(node // NC, NZL)
    x = lax.rem(node // (NC * NZL), NX)
    y = node // (NC * NZL * NX)
    z = z_hi * NZL + z_lo
    p = x * NC + core
    head_scale = float(HD) ** -0.5

    def device(y_, x_, core_):
        return (node_of(y_, x_, z_lo, core_), z_hi)

    sibling = device(y, x, 1 - core)
    x_peers = [lax.rem(x + d, NX) for d in range(1, NX)]
    y_peers = [lax.rem(y + d, NY) for d in range(1, NY)]
    far_peers = [lax.rem(z_hi + d, NZH) for d in range(1, NZH)]

    own_rows = w_hbm.at[pl.ds(pl.multiple_of(p * HD, HD), HD)]
    loads = [
        pltpu.make_async_copy(src, dst, load_sem.at[i])
        for i, (src, dst) in enumerate(
            [(q_hbm, q), (k_hbm, k), (g_hbm, g), (own_rows, w_cat.at[z_hi])]
        )
    ]
    for load in loads:
        load.start()

    barrier = pltpu.get_barrier_semaphore()

    def greet(device_id):
        pl.semaphore_signal(barrier, inc=1, device_id=device_id, device_id_type=MESH)

    giver_y, giver_x, giver_core = x * 2 + z_lo // 2, y // 2, lax.rem(y, 2)
    takes_own = (giver_y == y) & (giver_x == x) & (giver_core == core)
    for z_ in range(NZH * NZL):
        giver = (node_of(giver_y, giver_x, z_ % NZL, giver_core), z_ // NZL)

        @pl.when(jnp.logical_not(takes_own & (z == z_)))
        def _():
            greet(giver)

    for h in far_peers:
        greet((node, h))
    for y_ in y_peers:
        greet(device(y_, x, core))
    for x_ in x_peers:
        for core_ in (core, 1 - core):
            greet(device(y, x_, core_))
    greet(sibling)
    near = 1 + 2 * (NX - 1) + (NY - 1) + (NZH - 1)
    pl.semaphore_wait(barrier, near + NZH * NZL - jnp.where(takes_own, 1, 0))

    def send(src, dst, phase, device_id):
        pltpu.make_async_remote_copy(
            src_ref=src, dst_ref=dst, send_sem=send_sem.at[phase], recv_sem=recv_sem.at[phase],
            device_id=device_id, device_id_type=MESH,
        ).start()

    def wait(ref, sem):
        pltpu.make_async_copy(ref, ref, sem).wait()

    piece = w_hbm.at[pl.ds(pl.multiple_of(p * HD + y * 16, 16), 16)]
    for d, h in enumerate(far_peers):
        send(piece, w_far.at[y, NZH - 2 - d], W_Z, (node, h))

    def columns(zh, p_):
        return tok_hbm.at[:, pl.ds(pl.multiple_of(zh * (NG * HD) + p_ * HD, HD), HD)]

    def place(zh):
        return tok_group.at[zh // 2, p, :, (zh % 2) * HD : (zh % 2 + 1) * HD]

    def swap_tokens(zh):
        for x_ in x_peers:
            for core_ in (core, 1 - core):
                send(columns(zh, x_ * NC + core_), place(zh), TOK + zh, device(y, x_, core_))
        send(columns(zh, x * NC + 1 - core), place(zh), TOK + zh, sibling)
        pltpu.make_async_copy(columns(zh, p), place(zh), recv_sem.at[TOK + zh]).start()

    swap_tokens(0)

    key_ids = lax.broadcasted_iota(jnp.int32, (ROWS, 2 * ROWS), 0)
    lane_ids = lax.broadcasted_iota(jnp.int32, (ROWS, 2 * ROWS), 1)
    allowed = key_ids <= lax.rem(lane_ids, ROWS)
    exponent_scale = head_scale * LOG2_E

    def heads(ref, a, pair):
        first = a * GROUP + 2 * pair
        return jnp.concatenate(
            [ref[:, h * HD : (h + 1) * HD] for h in (first, first + 1)], axis=0
        )

    def softmax_head(a):
        cols = slice(a * HD, (a + 1) * HD)
        keys_a = k[:, cols]
        for pair in range(GROUP // 2):
            scores = over_columns(keys_a, heads(q, a, pair))
            scores = jnp.where(allowed, scores, F32(-1e30))
            peak = jnp.max(scores, axis=0, keepdims=True)
            raised = jnp.exp2((scores - peak) * exponent_scale)
            inverse = 1.0 / jnp.sum(raised, axis=0, keepdims=True)
            soft[a, :, pair * 2 * ROWS : (pair + 1) * 2 * ROWS] = (raised * inverse).astype(BF16)
        gv_group[a // 2, p, :, (a % 2) * HD : (a % 2 + 1) * HD] = jnp.dot(
            soft[a], stacked(g, a), preferred_element_type=F32
        ).astype(BF16)

    def share_grads(half):
        mine = gv_group.at[half, p]
        for x_ in x_peers:
            send(mine, mine, GV_X + half, device(y, x_, core))
        send(mine, mine, GV_OWN + half, sibling)

    def pass_grads(half):
        wait(gv_group.at[half, 0 : NX - 1], recv_sem.at[GV_X + half])
        for x_ in x_peers:
            theirs = gv_group.at[half, x_ * NC + core]
            send(theirs, theirs, GV_C + half, sibling)

    def turn_tokens(zh):
        wait(tok_group.at[0, 0 : NG // 2], recv_sem.at[TOK + zh])
        lanes = slice((zh % 2) * HD, (zh % 2 + 1) * HD)
        tok_turned[zh] = tok_group[zh // 2, :, :, lanes].reshape(NG * ROWS, HD).T

    for load in loads[:3]:
        load.wait()
    softmax_head(0)
    softmax_head(1)
    share_grads(0)
    softmax_head(2)
    softmax_head(3)
    share_grads(1)
    wait(w_far.at[0], recv_sem.at[W_Z])
    for y_ in y_peers:
        send(w_far.at[y], w_far.at[y], W_Y, device(y_, x, core))
    turn_tokens(0)
    pass_grads(0)
    swap_tokens(1)
    pass_grads(1)
    swap_tokens(2)
    swap_tokens(3)
    for half in range(2):
        wait(gv_group.at[half, 0], recv_sem.at[GV_OWN + half])
        wait(gv_group.at[half, 0 : NX - 1], recv_sem.at[GV_C + half])

    def term_rows(zh):
        for half in range(2):
            term = jnp.dot(
                tok_turned[zh], gv_group[half].reshape(NG * ROWS, KW // 2),
                preferred_element_type=F32,
            )
            term = (term * loss_scale).astype(BF16).reshape(NY, 16, KW // 2)
            part_send[zh, :, :, half * (KW // 2) : (half + 1) * (KW // 2)] = term
        for y_ in y_peers:
            send(part_send.at[zh, y_], part_recv.at[zh, y], PART + zh, device(y_, x, core))
        pltpu.make_async_copy(
            part_send.at[zh, y], part_recv.at[zh, y], recv_sem.at[PART + zh]
        ).start()

    def partial_values(pair, core_):
        left = jnp.concatenate([tok_group[pair, x_ * NC + core_] for x_ in range(NX)], axis=0)
        right = w_cat[2 * pair : 2 * pair + 2].reshape(2 * HD, KW)
        product = jnp.dot(left, right, preferred_element_type=F32)
        return product.reshape(NX, ROWS, KW)

    gives_own = (lax.rem(y, 2) == z_lo // 2) & (y // 2 == x) & (x * NC + core == y)

    def finish(zh):
        wait(part_recv.at[zh], recv_sem.at[PART + zh])
        part = part_recv[zh, 0].astype(F32)
        for y_ in range(1, NY):
            part = part + part_recv[zh, y_].astype(F32)
        for i in range(4):
            j = zh * 4 + i
            rows = part[4 * i : 4 * i + 4]
            fin_send[j] = jnp.concatenate(
                [rows[:, c * HD : (c + 1) * HD] for c in range(KW // HD)], axis=0
            ).astype(BF16)
            z_lo_, core_ = lax.rem(y, 2) * 2 + i // 2, i % 2
            owner = (node_of(x * NC + core, y // 2, z_lo_, core_), zh)
            own = gives_own & (z_hi == zh) & (z_lo == z_lo_) & (core == core_)

            @pl.when(own)
            def _():
                pltpu.make_async_copy(fin_send.at[j], fin_recv.at[z], recv_sem.at[FIN]).start()

            @pl.when(jnp.logical_not(own))
            def _():
                send(fin_send.at[j], fin_recv.at[z], FIN, owner)

    term_rows(0)
    wait(w_far.at[0 : NY - 1], recv_sem.at[W_Y])
    loads[3].wait()
    for d, h in enumerate(far_peers):
        w_cat[h] = w_far[:, d].reshape(HD, KW)
    turn_tokens(1)
    term_rows(1)
    val_other[...] = partial_values(0, 1 - core)
    val_own[...] = partial_values(0, core)
    turn_tokens(2)
    term_rows(2)
    finish(0)
    turn_tokens(3)
    term_rows(3)
    pair_send[...] = (val_other[...] + partial_values(1, 1 - core)).astype(BF16)
    for i, x_ in enumerate(x_peers + [x]):
        send(pair_send.at[x_], pair_recv.at[x_], PAIR + i, sibling)
    val_own[...] = val_own[...] + partial_values(1, core)

    for i, x_ in enumerate(x_peers):
        wait(pair_recv.at[x_], recv_sem.at[PAIR + i])
        val_send[x_] = (val_own[x_] + pair_recv[x_].astype(F32)).astype(BF16)
        for half in range(2):
            lanes = slice(half * (KW // 2), (half + 1) * (KW // 2))
            send(
                val_send.at[x_, :, lanes], val_recv.at[half, x], VAL + half, device(y, x_, core)
            )
    finish(1)
    finish(2)
    finish(3)

    wait(pair_recv.at[x], recv_sem.at[PAIR + NX - 1])
    for half in range(2):
        lanes = slice(half * (KW // 2), (half + 1) * (KW // 2))
        total = val_own[x, :, lanes] + pair_recv[x, :, lanes].astype(F32)
        wait(val_recv.at[half, 0 : NX - 1], recv_sem.at[VAL + half])
        for x_ in x_peers:
            total = total + val_recv[half, x_].astype(F32)
        values = total.astype(BF16)
        for a in (2 * half, 2 * half + 1):
            values_a = values[:, (a % 2) * HD : (a % 2 + 1) * HD]
            grad_scores = []
            for pair in range(GROUP // 2):
                grad_probs = over_columns(values_a, heads(g, a, pair))
                soft_float = soft[a, :, pair * 2 * ROWS : (pair + 1) * 2 * ROWS].astype(F32)
                delta = jnp.sum(soft_float * grad_probs, axis=0, keepdims=True)
                grad_scores.append((soft_float * (grad_probs - delta)).astype(BF16))
            d_keys = jnp.dot(
                jnp.concatenate(grad_scores, axis=1), stacked(q, a), preferred_element_type=F32
            )
            dk_ref[:, a * HD : (a + 1) * HD] = (d_keys * head_scale).astype(BF16)

    wait(fin_recv, recv_sem.at[FIN])
    out = fin_recv[0].astype(F32)
    for z_ in range(1, NZH * NZL):
        out = out + fin_recv[z_].astype(F32)
    for c in range(KW // HD):
        gw_ref[:, c * HD : (c + 1) * HD] = out[4 * c : 4 * c + 4]

    wait(w_far.at[0], send_sem.at[W_Z])
    wait(w_far.at[0 : NY - 1], send_sem.at[W_Y])
    for zh in range(NZH):
        wait(gv_group.at[0, 0:7, :, 0:128], send_sem.at[TOK + zh])
        wait(part_send.at[zh, 0 : NY - 1], send_sem.at[PART + zh])
    for half in range(2):
        wait(gv_group.at[half, 0 : NX - 1], send_sem.at[GV_X + half])
        wait(gv_group.at[half, 0], send_sem.at[GV_OWN + half])
        wait(gv_group.at[half, 0 : NX - 1], send_sem.at[GV_C + half])
        wait(val_recv.at[half, 0 : NX - 1], send_sem.at[VAL + half])
    for i in range(NX):
        wait(pair_send.at[0], send_sem.at[PAIR + i])
    wait(fin_send.at[0:15], send_sem.at[FIN])

    @pl.when(jnp.logical_not(gives_own))
    def _():
        wait(fin_send.at[0], send_sem.at[FIN])


def shards(tokens, queries, keys, grad_attended, w_value):
    total_tokens = lax.axis_size("node") * lax.axis_size("local") * tokens.shape[0]
    loss_scale = float(total_tokens) ** -0.5

    def body(*refs):
        kernel(*refs, loss_scale=loss_scale)

    return pl.pallas_call(
        body,
        out_shape=(
            pltpu.VMEM((ROWS, KW), BF16),
            pltpu.VMEM((4, KW), F32),
        ),
        in_specs=[pl.BlockSpec(memory_space=pl.ANY)] * 5,
        out_specs=(pl.BlockSpec(memory_space=pltpu.VMEM),) * 2,
        scratch_shapes=[
            pltpu.VMEM((ROWS, 4096), BF16),
            pltpu.VMEM((ROWS, KW), BF16),
            pltpu.VMEM((ROWS, 4096), BF16),
            pltpu.VMEM((NY, NZH - 1, 16, KW), BF16),
            pltpu.VMEM((NZH, HD, KW), BF16),
            pltpu.VMEM((KVH, ROWS, GROUP * ROWS), BF16),
            pltpu.VMEM((2, NG, ROWS, 2 * HD), BF16),
            pltpu.VMEM((NZH, HD, NG * ROWS), BF16),
            pltpu.VMEM((2, NG, ROWS, KW // 2), BF16),
            pltpu.VMEM((NZH, NY, 16, KW), BF16),
            pltpu.VMEM((NZH, NY, 16, KW), BF16),
            pltpu.VMEM((16, 16, HD), BF16),
            pltpu.VMEM((16, 16, HD), BF16),
            pltpu.VMEM((NX, ROWS, KW), BF16),
            pltpu.VMEM((NX, ROWS, KW), BF16),
            pltpu.VMEM((NX, ROWS, KW), F32),
            pltpu.VMEM((NX, ROWS, KW), F32),
            pltpu.VMEM((NX, ROWS, KW), BF16),
            pltpu.VMEM((2, NX, ROWS, KW // 2), BF16),
            pltpu.SemaphoreType.DMA((4,)),
            pltpu.SemaphoreType.DMA((23,)),
            pltpu.SemaphoreType.DMA((23,)),
        ],
        compiler_params=pltpu.CompilerParams(
            collective_id=0, has_side_effects=True, vmem_limit_bytes=60 * 1024 * 1024
        ),
        cost_estimate=pl.CostEstimate(
            flops=1_700_000_000, bytes_accessed=5_000_000, transcendentals=524_288
        ),
    )(tokens, queries, keys, grad_attended, w_value)


def solution(mesh):
    in_specs = (
        P(("node", "local"), None),
        P(("node", "local"), None),
        P(("node", "local"), None),
        P(("node", "local"), None),
        P("local", None),
    )
    out_specs = (P(("node", "local"), None), P(("local", "node"), None))
    return jax.shard_map(shards, mesh=mesh, in_specs=in_specs, out_specs=out_specs, check_vma=False)
```

time: 67.9 us -> 64.3 us (0.947)
  the two profiles are of different devices: /device:TPU:1 before, /device:TPU:241 now
where the time goes in v3:
time: 64.3 us; the launch traced here: 64.1 us
  Pallas kernels  62.2 us (97%)
  local copies, waits for them, and re-layouts  1.26 us (2%)
    pallas_call x1, Pallas kernels, shards(): pl.pallas_call(body, out_shape=(pltpu.VMEM((ROWS, KW), BF16), pltpu.VMEM(...  62.2 us

profile of v3, /device:TPU:241, one launch (start us, length us, event | category | flops | bytes accessed | tf_op | source)
XLA Modules:
  0.0 64.1 jit_solution(9028575942351022377)
XLA Ops:
  0.6 62.2 %shard_map.68 = (bf16[128,512]{1,0:T(8,128)(2,1)S(1)}, f32[4,512]{1,0:T(4,128)S(1)}) custom-call(bf16[128,4096]{1,0:T(8,128)(2,1)} %refs_0_.1, bf16[128,4096]{1,0:T(8,128)(2,1)} %refs_1_.1, bf16[128,512]{1,0:T(8,128)(2,1)} %refs_2_.1, bf16[128,4096]{1,0:T(8,128)(2,1)} %refs_3_.1, bf16[1024,512]{1,0:T(8,128)(2,1)} %refs_4_.1), custom_call_target="tpu_custom_call" | custom-call | flops 1700000000 | bytes 5000000 | tf_op jit(solution)/shard_map/pallas_call | solution.py:315
  62.9 0.7 %copy.9 = bf16[128,512]{1,0:T(8,128)(2,1)} copy(bf16[128,512]{1,0:T(8,128)(2,1)S(1)} %get-tuple-element.2) | data formatting | bytes 262144
  63.5 0.6 copy.10

commit v4 on v3

--- a/solution.py
+++ b/solution.py
@@ -12,7 +12,7 @@
 KW = 512
 NX, NY, NZL, NZH, NC = 4, 8, 4, 4, 2
 NG = NX * NC
-W_Z, W_Y, FIN, GV_X, GV_OWN, GV_C, VAL, TOK, PART, PAIR = 0, 1, 2, 3, 5, 7, 9, 11, 15, 19
+W_Z, W_L, FIN, GV_X, GV_OWN, GV_C, VAL, TOK, PART, PAIR = 0, 1, 2, 3, 5, 7, 9, 11, 15, 19
 LOG2_E = 1.4426950408889634
 MESH = pl.DeviceIdType.MESH
 F32 = jnp.float32
@@ -36,7 +36,7 @@
 def kernel(
     tok_hbm, q_hbm, k_hbm, g_hbm, w_hbm, dk_ref, gw_ref,
     q, k, g, w_far, w_cat, soft, tok_group, tok_turned, gv_group, part_send, part_recv,
-    fin_send, fin_recv, pair_send, pair_recv, val_own, val_other, val_send, val_recv,
+    fin_send, fin_recv, pair_send, pair_recv, val_own, val_send, val_recv,
     load_sem, send_sem, recv_sem, *, loss_scale,
 ):
     node, z_hi = lax.axis_index("node"), lax.axis_index("local")
@@ -54,6 +54,7 @@
     sibling = device(y, x, 1 - core)
     x_peers = [lax.rem(x + d, NX) for d in range(1, NX)]
     y_peers = [lax.rem(y + d, NY) for d in range(1, NY)]
+    line_peers = [lax.rem(z_lo + d, NZL) for d in range(1, NZL)]
     far_peers = [lax.rem(z_hi + d, NZH) for d in range(1, NZH)]
 
     own_rows = w_hbm.at[pl.ds(pl.multiple_of(p * HD, HD), HD)]
@@ -82,13 +83,15 @@
 
     for h in far_peers:
         greet((node, h))
+    for z_lo_ in line_peers:
+        greet((node_of(y, x, z_lo_, core), z_hi))
     for y_ in y_peers:
         greet(device(y_, x, core))
     for x_ in x_peers:
         for core_ in (core, 1 - core):
             greet(device(y, x_, core_))
     greet(sibling)
-    near = 1 + 2 * (NX - 1) + (NY - 1) + (NZH - 1)
+    near = 1 + 2 * (NX - 1) + (NY - 1) + (NZH - 1) + (NZL - 1)
     pl.semaphore_wait(barrier, near + NZH * NZL - jnp.where(takes_own, 1, 0))
 
     def send(src, dst, phase, device_id):
@@ -100,9 +103,9 @@
     def wait(ref, sem):
         pltpu.make_async_copy(ref, ref, sem).wait()
 
-    piece = w_hbm.at[pl.ds(pl.multiple_of(p * HD + y * 16, 16), 16)]
+    piece = w_hbm.at[pl.ds(pl.multiple_of(p * HD + z_lo * 32, 32), 32)]
     for d, h in enumerate(far_peers):
-        send(piece, w_far.at[y, NZH - 2 - d], W_Z, (node, h))
+        send(piece, w_far.at[z_lo, NZH - 2 - d], W_Z, (node, h))
 
     def columns(zh, p_):
         return tok_hbm.at[:, pl.ds(pl.multiple_of(zh * (NG * HD) + p_ * HD, HD), HD)]
@@ -170,8 +173,8 @@
     softmax_head(3)
     share_grads(1)
     wait(w_far.at[0], recv_sem.at[W_Z])
-    for y_ in y_peers:
-        send(w_far.at[y], w_far.at[y], W_Y, device(y_, x, core))
+    for z_lo_ in line_peers:
+        send(w_far.at[z_lo], w_far.at[z_lo], W_L, (node_of(y, x, z_lo_, core), z_hi))
     turn_tokens(0)
     pass_grads(0)
     swap_tokens(1)
@@ -196,11 +199,14 @@
             part_send.at[zh, y], part_recv.at[zh, y], recv_sem.at[PART + zh]
         ).start()
 
-    def partial_values(pair, core_):
-        left = jnp.concatenate([tok_group[pair, x_ * NC + core_] for x_ in range(NX)], axis=0)
-        right = w_cat[2 * pair : 2 * pair + 2].reshape(2 * HD, KW)
-        product = jnp.dot(left, right, preferred_element_type=F32)
-        return product.reshape(NX, ROWS, KW)
+    def partial_values(core_):
+        total = None
+        for pair in range(2):
+            left = jnp.concatenate([tok_group[pair, x_ * NC + core_] for x_ in range(NX)], axis=0)
+            right = w_cat[2 * pair : 2 * pair + 2].reshape(2 * HD, KW)
+            product = jnp.dot(left, right, preferred_element_type=F32)
+            total = product if total is None else total + product
+        return total.reshape(NX, ROWS, KW)
 
     gives_own = (lax.rem(y, 2) == z_lo // 2) & (y // 2 == x) & (x * NC + core == y)
 
@@ -228,23 +234,21 @@
                 send(fin_send.at[j], fin_recv.at[z], FIN, owner)
 
     term_rows(0)
-    wait(w_far.at[0 : NY - 1], recv_sem.at[W_Y])
-    loads[3].wait()
-    for d, h in enumerate(far_peers):
-        w_cat[h] = w_far[:, d].reshape(HD, KW)
     turn_tokens(1)
     term_rows(1)
-    val_other[...] = partial_values(0, 1 - core)
-    val_own[...] = partial_values(0, core)
     turn_tokens(2)
     term_rows(2)
     finish(0)
     turn_tokens(3)
     term_rows(3)
-    pair_send[...] = (val_other[...] + partial_values(1, 1 - core)).astype(BF16)
+    wait(w_far.at[0 : NZL - 1], recv_sem.at[W_L])
+    loads[3].wait()
+    for d, h in enumerate(far_peers):
+        w_cat[h] = w_far[:, d].reshape(HD, KW)
+    pair_send[...] = partial_values(1 - core).astype(BF16)
     for i, x_ in enumerate(x_peers + [x]):
         send(pair_send.at[x_], pair_recv.at[x_], PAIR + i, sibling)
-    val_own[...] = val_own[...] + partial_values(1, core)
+    val_own[...] = partial_values(core)
 
     for i, x_ in enumerate(x_peers):
         wait(pair_recv.at[x_], recv_sem.at[PAIR + i])
@@ -287,7 +291,7 @@
         gw_ref[:, c * HD : (c + 1) * HD] = out[4 * c : 4 * c + 4]
 
     wait(w_far.at[0], send_sem.at[W_Z])
-    wait(w_far.at[0 : NY - 1], send_sem.at[W_Y])
+    wait(w_far.at[0 : NZL - 1], send_sem.at[W_L])
     for zh in range(NZH):
         wait(gv_group.at[0, 0:7, :, 0:128], send_sem.at[TOK + zh])
         wait(part_send.at[zh, 0 : NY - 1], send_sem.at[PART + zh])
@@ -324,7 +328,7 @@
             pltpu.VMEM((ROWS, 4096), BF16),
             pltpu.VMEM((ROWS, KW), BF16),
             pltpu.VMEM((ROWS, 4096), BF16),
-            pltpu.VMEM((NY, NZH - 1, 16, KW), BF16),
+            pltpu.VMEM((NZL, NZH - 1, 32, KW), BF16),
             pltpu.VMEM((NZH, HD, KW), BF16),
             pltpu.VMEM((KVH, ROWS, GROUP * ROWS), BF16),
             pltpu.VMEM((2, NG, ROWS, 2 * HD), BF16),
@@ -336,7 +340,6 @@
             pltpu.VMEM((16, 16, HD), BF16),
             pltpu.VMEM((NX, ROWS, KW), BF16),
             pltpu.VMEM((NX, ROWS, KW), BF16),
-            pltpu.VMEM((NX, ROWS, KW), F32),
             pltpu.VMEM((NX, ROWS, KW), F32),
             pltpu.VMEM((NX, ROWS, KW), BF16),
             pltpu.VMEM((2, NX, ROWS, KW // 2), BF16),

time: 64.3 us -> 60.6 us (0.942)
  the two profiles are of different devices: /device:TPU:241 before, /device:TPU:71 now
where the time goes in v4:
time: 60.6 us; the launch traced here: 60.5 us
  Pallas kernels  58.6 us (97%)
  local copies, waits for them, and re-layouts  1.26 us (2%)
  between operations  0.64 us (1%)
    pallas_call x1, Pallas kernels, shards(): pl.pallas_call(body, out_shape=(pltpu.VMEM((ROWS, KW), BF16), pltpu.VMEM(...  58.6 us
    unnamed x2, local copies, waits for them, and re-layouts  1.26 us

profile of v4, /device:TPU:71, one launch (start us, length us, event | category | flops | bytes accessed | tf_op | source)
XLA Modules:
  0.0 60.5 jit_solution(6193135685147259560)
XLA Ops:
  0.6 58.6 %shard_map.68 = (bf16[128,512]{1,0:T(8,128)(2,1)S(1)}, f32[4,512]{1,0:T(4,128)S(1)}) custom-call(bf16[128,4096]{1,0:T(8,128)(2,1)} %refs_0_.1, bf16[128,4096]{1,0:T(8,128)(2,1)} %refs_1_.1, bf16[128,512]{1,0:T(8,128)(2,1)} %refs_2_.1, bf16[128,4096]{1,0:T(8,128)(2,1)} %refs_3_.1, bf16[1024,512]{1,0:T(8,128)(2,1)} %refs_4_.1), custom_call_target="tpu_custom_call" | custom-call | flops 1700000000 | bytes 5000000 | tf_op jit(solution)/shard_map/pallas_call | solution.py:319
  59.2 0.7 %copy.9 = bf16[128,512]{1,0:T(8,128)(2,1)} copy(bf16[128,512]{1,0:T(8,128)(2,1)S(1)} %get-tuple-element.2) | data formatting | bytes 262144
  59.9 0.6 copy.10

commit v5 on v4

--- a/solution.py
+++ b/solution.py
@@ -172,12 +172,12 @@
     softmax_head(2)
     softmax_head(3)
     share_grads(1)
+    swap_tokens(1)
     wait(w_far.at[0], recv_sem.at[W_Z])
     for z_lo_ in line_peers:
         send(w_far.at[z_lo], w_far.at[z_lo], W_L, (node_of(y, x, z_lo_, core), z_hi))
     turn_tokens(0)
     pass_grads(0)
-    swap_tokens(1)
     pass_grads(1)
     swap_tokens(2)
     swap_tokens(3)

time: 60.6 us -> 59.6 us (0.983)
  the two profiles are of different devices: /device:TPU:71 before, /device:TPU:1 now
where the time goes in v5:
time: 59.6 us; the launch traced here: 59.5 us
  Pallas kernels  57.6 us (97%)
  local copies, waits for them, and re-layouts  1.26 us (2%)
  between operations  0.64 us (1%)
    pallas_call x1, Pallas kernels, shards(): pl.pallas_call(body, out_shape=(pltpu.VMEM((ROWS, KW), BF16), pltpu.VMEM(...  57.6 us
    unnamed x2, local copies, waits for them, and re-layouts  1.26 us

profile of v5, /device:TPU:1, one launch (start us, length us, event | category | flops | bytes accessed | tf_op | source)
XLA Modules:
  0.0 59.5 jit_solution(17412616085411323660)
XLA Ops:
  0.6 57.6 %shard_map.68 = (bf16[128,512]{1,0:T(8,128)(2,1)S(1)}, f32[4,512]{1,0:T(4,128)S(1)}) custom-call(bf16[128,4096]{1,0:T(8,128)(2,1)} %refs_0_.1, bf16[128,4096]{1,0:T(8,128)(2,1)} %refs_1_.1, bf16[128,512]{1,0:T(8,128)(2,1)} %refs_2_.1, bf16[128,4096]{1,0:T(8,128)(2,1)} %refs_3_.1, bf16[1024,512]{1,0:T(8,128)(2,1)} %refs_4_.1), custom_call_target="tpu_custom_call" | custom-call | flops 1700000000 | bytes 5000000 | tf_op jit(solution)/shard_map/pallas_call | solution.py:319
  58.2 0.7 %copy.9 = bf16[128,512]{1,0:T(8,128)(2,1)} copy(bf16[128,512]{1,0:T(8,128)(2,1)S(1)} %get-tuple-element.2) | data formatting | bytes 262144
  58.9 0.6 %copy.10 = f32[4,512]{1,0:T(4,128)} copy(f32[4,512]{1,0:T(4,128)S(1)} %get-tuple-element.3) | data formatting | bytes 16384

commit v6 on v5

--- a/solution.py
+++ b/solution.py
@@ -52,7 +52,7 @@
         return (node_of(y_, x_, z_lo, core_), z_hi)
 
     sibling = device(y, x, 1 - core)
-    x_peers = [lax.rem(x + d, NX) for d in range(1, NX)]
+    x_peers = [lax.rem(x + d, NX) for d in (2, 1, 3)]
     y_peers = [lax.rem(y + d, NY) for d in range(1, NY)]
     line_peers = [lax.rem(z_lo + d, NZL) for d in range(1, NZL)]
     far_peers = [lax.rem(z_hi + d, NZH) for d in range(1, NZH)]

time: 59.6 us -> 60.2 us (1.010)
  no operation moved by 1% of the time
where the time goes in v6:
time: 60.2 us; the launch traced here: 60 us
  Pallas kernels  58.1 us (97%)
  local copies, waits for them, and re-layouts  1.26 us (2%)
  between operations  0.64 us (1%)
    pallas_call x1, Pallas kernels, shards(): pl.pallas_call(body, out_shape=(pltpu.VMEM((ROWS, KW), BF16), pltpu.VMEM(...  58.1 us
    unnamed x2, local copies, waits for them, and re-layouts  1.26 us

profile of v6, /device:TPU:1, one launch (start us, length us, event | category | flops | bytes accessed | tf_op | source)
XLA Modules:
  0.0 60.0 jit_solution(12017802734991923706)
XLA Ops:
  0.6 58.1 %shard_map.68 = (bf16[128,512]{1,0:T(8,128)(2,1)S(1)}, f32[4,512]{1,0:T(4,128)S(1)}) custom-call(bf16[128,4096]{1,0:T(8,128)(2,1)} %refs_0_.1, bf16[128,4096]{1,0:T(8,128)(2,1)} %refs_1_.1, bf16[128,512]{1,0:T(8,128)(2,1)} %refs_2_.1, bf16[128,4096]{1,0:T(8,128)(2,1)} %refs_3_.1, bf16[1024,512]{1,0:T(8,128)(2,1)} %refs_4_.1), custom_call_target="tpu_custom_call" | custom-call | flops 1700000000 | bytes 5000000 | tf_op jit(solution)/shard_map/pallas_call | solution.py:319
  58.8 0.7 %copy.9 = bf16[128,512]{1,0:T(8,128)(2,1)} copy(bf16[128,512]{1,0:T(8,128)(2,1)S(1)} %get-tuple-element.2) | data formatting | bytes 262144
  59.4 0.6 copy.10
